TPU v7x, 32 devices: a whole 2x2x4 slice. The times are simulated.
32 devices in a mesh: row: 4 (over y, core), col: 8 (over z, x).
Axes of the slice: x: 2, y: 2, z: 4, core: 2. Of those that a mesh axis runs over, the one named last changes fastest.
Arguments:
- row_gen: bfloat16 [64, 1024, 256], P(('row', 'col')), may hold values from -6 to 6
- row_upd: bfloat16 [64, 1024, 256], P(('row', 'col')), may hold values from -6 to 6
- col_gen: bfloat16 [64, 1024, 256], P('row', 'col'), may hold values from -6 to 6
- col_upd: bfloat16 [64, 1024, 256], P('row', 'col'), may hold values from -6 to 6
- leaf_rank: int32 [64], P(('row', 'col')), may hold values from 32 to 256, as said below
- leaf_trunc: int32 [64], P(('row', 'col')), may hold values from 128 to 512
- node_trunc: int32 [4, 14], replicated, may hold values from 128 to 384, as said below
- coupling: float32 [2048, 512], P(('row', 'col')), may hold values from -6 to 6
Outputs:
- recompressed: float32 [2048, 512], P(('row', 'col'))
Inputs may be any that keep to these rules, and one draw needn't show every extreme that they name: `leaf_rank`: the first leaf of every device (leaf indices that are multiples of 2) has rank 256. `node_trunc`: column 0 (the first height-0 node of each top node) is 384 in every row.
All inputs are finite; a program needn't handle non-finite values.
Results may differ from a plain program's by a relative error of at most 0.0003.
Values may be sent and summed in bfloat16 or wider, within the bound.
A program may use at most 128 MiB of HBM per device.

v0:
```python
import jax
import jax.numpy as jnp
from jax import lax
from jax.sharding import PartitionSpec as P

HIGH = lax.Precision.HIGHEST
OFFSETS = (0, 8, 12)


def partner(block, axis, distance):
    count = lax.axis_size(axis)
    route = []
    for low in range(count):
        high = low | 1 << distance
        if high != low and high < count:
            route += [(low, high), (high, low)]
    return lax.ppermute(block, axis, route)


def both_factors(generators, updates, ranks, truncs):
    leaf_count = ranks.shape[0] // 2
    width_gen = generators.shape[2]
    col_ids = lax.broadcasted_iota(jnp.int32, (1, 1, width_gen), 2)
    keep_cols = (col_ids < ranks[:, None, None]).astype(generators.dtype)
    stacked = jnp.concatenate([generators * keep_cols, updates], axis=2)
    gram_matrix = jnp.einsum("nlk,nlm->nkm", stacked, stacked, preferred_element_type=jnp.float32)
    width_all = gram_matrix.shape[1]
    gram_matrix = gram_matrix + jnp.eye(width_all, dtype=jnp.float32)
    factor = jnp.swapaxes(jnp.linalg.cholesky(gram_matrix), 1, 2)
    row_ids = lax.broadcasted_iota(jnp.int32, (1, width_all, 1), 1)
    kept_rows = factor * (row_ids < truncs[:, None, None]).astype(jnp.float32)
    kept_rows = kept_rows.reshape(2, leaf_count * width_all, width_all)
    node_gram = jnp.einsum("srk,srm->skm", kept_rows, kept_rows, precision=HIGH) + jnp.eye(
        width_all, dtype=jnp.float32
    )
    return jnp.swapaxes(jnp.linalg.cholesky(node_gram), 1, 2)


def truncate(factors, keep_rank):
    row_ids = lax.broadcasted_iota(jnp.int32, (1, factors.shape[1], 1), 1)
    return factors * (row_ids < keep_rank).astype(jnp.float32)


def merge_pair(own_rows, other_rows):
    width_all = own_rows.shape[2]
    gram_matrix = jnp.einsum("srk,srm->skm", own_rows, own_rows, precision=HIGH)
    gram_matrix = gram_matrix + jnp.einsum("srk,srm->skm", other_rows, other_rows, precision=HIGH)
    gram_matrix = gram_matrix + jnp.eye(width_all, dtype=jnp.float32)
    return jnp.swapaxes(jnp.linalg.cholesky(gram_matrix), 1, 2)


def body(row_gen, row_upd, col_gen, col_upd, leaf_rank, leaf_trunc, node_trunc, coupling):
    col_gen_full, col_upd_full = (
        lax.all_to_all(col_gen, "col", split_axis=0, concat_axis=1, tiled=True),
        lax.all_to_all(col_upd, "col", split_axis=0, concat_axis=1, tiled=True),
    )
    generators = jnp.concatenate([row_gen, col_gen_full], 0)
    updates = jnp.concatenate([row_upd, col_upd_full], 0)
    ranks = jnp.concatenate([leaf_rank, leaf_rank], 0)
    truncs = jnp.concatenate([leaf_trunc, leaf_trunc], 0)
    factors = both_factors(generators, updates, ranks, truncs)
    row_pos = lax.axis_index("row")
    col_pos = lax.axis_index("col")
    groups = lax.axis_size("col") // 8
    top_node = row_pos * groups + col_pos // 8
    member = col_pos % 8
    width_all = factors.shape[1]
    for height in range(3):
        keep_rank = node_trunc[top_node, OFFSETS[height] + (member >> height)]
        kept = truncate(factors, keep_rank)
        row_other, col_other = partner((kept[0], kept[1]), "col", height)
        factors = merge_pair(kept, jnp.stack([row_other, col_other], 0))
    row_factor = factors[0]
    col_factor = factors[1]
    partner_col = partner(col_factor, "row", 0)
    share_rows = width_all // 8
    my_rows = lax.dynamic_slice_in_dim(row_factor, member * share_rows, share_rows, 0)
    group_start = col_pos // 8 * width_all
    piece_rows = lax.all_gather(coupling, "col", axis=0, tiled=True)
    row_count = piece_rows.shape[0]
    positions = lax.broadcasted_iota(jnp.int32, (row_count,), 0) - group_start
    inside = (positions >= 0) & (positions < width_all)
    picked = jnp.take(my_rows, jnp.clip(positions, 0, width_all - 1), axis=1)
    picked = picked * inside.astype(jnp.float32)[None, :]
    projected = jnp.dot(picked, piece_rows, precision=HIGH)
    result = jnp.dot(projected, partner_col.T, precision=HIGH)
    return result / (8 * row_gen.shape[0] * row_gen.shape[1])


def solution(mesh):
    return jax.shard_map(
        body,
        mesh=mesh,
        in_specs=(
            P(("row", "col"), None, None),
            P(("row", "col"), None, None),
            P("row", "col", None),
            P("row", "col", None),
            P(("row", "col")),
            P(("row", "col")),
            P(),
            P(("row", "col"), None),
        ),
        out_specs=P(("row", "col"), None),
        check_vma=False,
    )
```

profile of v0, /device:TPU:0, one launch (start us, length us, event | category | flops | bytes accessed | tf_op | source)
XLA Modules:
  0.0 1381.0 jit_solution(1498919530769658933)
XLA Ops:
  6.5 33.1 %all_to_all.36 = bf16[16,128,256]{2,1,0:T(8,128)(2,1)} all-to-all(bf16[16,128,256]{2,1,0:T(8,128)(2,1)} %param.11), channel_id=1, replica_groups=mesh['row'=4,'col'=8] {'col'}, dimensions={0} | all-to-all | bytes 2097152 | tf_op jit(solution)/shard_map/all_to_all | solution.py:54
  88.7 46.9 %custom-call.55 = f32[4,128,128]{2,1,0:T(8,128)S(1)} custom-call(f32[4,128,128]{2,1,0:T(8,128)S(1)} %cholesky.1016), custom_call_target="Cholesky" | custom-call | tf_op jit(solution)/shard_map/jit(cholesky)/cholesky | solution.py:29
  135.7 39.3 %custom-call.56 = f32[4,1,128,128]{2,3,1,0:T(8,128)S(1)} custom-call(f32[4,1,128,128]{3,2,1,0:T(8,128)S(1)} %select_bitcast_fusion.3), custom_call_target="InvertDiagBlocksLowerTriangular" | custom-call | tf_op jit(solution)/shard_map/jit(cholesky)/cholesky | solution.py:29
  183.4 47.9 %custom-call.57 = f32[4,128,128]{2,1,0:T(8,128)S(1)} custom-call(f32[4,128,128]{2,1,0:T(8,128)} %cholesky.1020), custom_call_target="Cholesky" | custom-call | tf_op jit(solution)/shard_map/jit(cholesky)/cholesky | solution.py:29
  233.1 39.3 %custom-call.58 = f32[4,1,128,128]{2,3,1,0:T(8,128)S(1)} custom-call(f32[4,1,128,128]{3,2,1,0:T(8,128)S(1)} %get-tuple-element.37), custom_call_target="InvertDiagBlocksLowerTriangular" | custom-call | tf_op jit(solution)/shard_map/jit(cholesky)/cholesky | solution.py:29
  276.5 46.9 %custom-call.59 = f32[4,128,128]{2,1,0:T(8,128)S(1)} custom-call(f32[4,128,128]{2,1,0:T(8,128)S(1)} %cholesky.1025), custom_call_target="Cholesky" | custom-call | tf_op jit(solution)/shard_map/jit(cholesky)/cholesky | solution.py:29
  324.2 39.5 %custom-call.60 = f32[4,1,128,128]{2,3,1,0:T(8,128)S(1)} custom-call(f32[4,1,128,128]{3,2,1,0:T(8,128)S(1)} %get-tuple-element.35), custom_call_target="InvertDiagBlocksLowerTriangular" | custom-call | tf_op jit(solution)/shard_map/jit(cholesky)/cholesky | solution.py:29
  367.5 46.9 %custom-call.61 = f32[4,128,128]{2,1,0:T(8,128)S(1)} custom-call(f32[4,128,128]{2,1,0:T(8,128)S(1)} %convolution_subtract_fusion.10), custom_call_target="Cholesky" | custom-call | tf_op jit(solution)/shard_map/jit(cholesky)/cholesky | solution.py:29
  441.8 23.5 %custom-call.83 = f32[2,128,128]{2,1,0:T(8,128)S(1)} custom-call(f32[2,128,128]{2,1,0:T(8,128)S(1)} %cholesky.1029), custom_call_target="Cholesky" | custom-call | tf_op jit(solution)/shard_map/jit(cholesky)/cholesky | solution.py:36
  491.7 25.0 %custom-call.85 = f32[2,128,128]{2,1,0:T(8,128)} custom-call(f32[2,128,128]{2,1,0:T(8,128)} %cholesky.1033), custom_call_target="Cholesky" | custom-call | tf_op jit(solution)/shard_map/jit(cholesky)/cholesky | solution.py:36
  543.8 24.9 %custom-call.87 = f32[2,128,128]{2,1,0:T(8,128)} custom-call(f32[2,128,128]{2,1,0:T(8,128)} %cholesky.1038), custom_call_target="Cholesky" | custom-call | tf_op jit(solution)/shard_map/jit(cholesky)/cholesky | solution.py:36
  594.9 25.3 %custom-call.89 = f32[2,128,128]{2,1,0:T(8,128)} custom-call(f32[2,128,128]{2,1,0:T(8,128)} %convolution_subtract_fusion.14), custom_call_target="Cholesky" | custom-call | tf_op jit(solution)/shard_map/jit(cholesky)/cholesky | solution.py:36
  678.1 23.6 %custom-call.90 = f32[2,128,128]{2,1,0:T(8,128)S(1)} custom-call(f32[2,128,128]{2,1,0:T(8,128)S(1)} %cholesky.1042), custom_call_target="Cholesky" | custom-call | tf_op jit(solution)/shard_map/jit(cholesky)/cholesky | solution.py:49
  728.2 24.9 %custom-call.92 = f32[2,128,128]{2,1,0:T(8,128)} custom-call(f32[2,128,128]{2,1,0:T(8,128)} %cholesky.1046), custom_call_target="Cholesky" | custom-call | tf_op jit(solution)/shard_map/jit(cholesky)/cholesky | solution.py:49
  780.3 24.9 %custom-call.94 = f32[2,128,128]{2,1,0:T(8,128)} custom-call(f32[2,128,128]{2,1,0:T(8,128)} %cholesky.1051), custom_call_target="Cholesky" | custom-call | tf_op jit(solution)/shard_map/jit(cholesky)/cholesky | solution.py:49
  831.3 25.3 %custom-call.96 = f32[2,128,128]{2,1,0:T(8,128)} custom-call(f32[2,128,128]{2,1,0:T(8,128)} %convolution_subtract_fusion.13), custom_call_target="Cholesky" | custom-call | tf_op jit(solution)/shard_map/jit(cholesky)/cholesky | solution.py:49
  913.5 23.6 %custom-call.97 = f32[2,128,128]{2,1,0:T(8,128)S(1)} custom-call(f32[2,128,128]{2,1,0:T(8,128)S(1)} %cholesky.1055), custom_call_target="Cholesky" | custom-call | tf_op jit(solution)/shard_map/jit(cholesky)/cholesky | solution.py:49
  963.6 24.9 %custom-call.99 = f32[2,128,128]{2,1,0:T(8,128)} custom-call(f32[2,128,128]{2,1,0:T(8,128)} %cholesky.1059), custom_call_target="Cholesky" | custom-call | tf_op jit(solution)/shard_map/jit(cholesky)/cholesky | solution.py:49
  1015.7 24.9 %custom-call.101 = f32[2,128,128]{2,1,0:T(8,128)} custom-call(f32[2,128,128]{2,1,0:T(8,128)} %cholesky.1064), custom_call_target="Cholesky" | custom-call | tf_op jit(solution)/shard_map/jit(cholesky)/cholesky | solution.py:49
  1066.7 25.3 %custom-call.103 = f32[2,128,128]{2,1,0:T(8,128)} custom-call(f32[2,128,128]{2,1,0:T(8,128)} %convolution_subtract_fusion.12), custom_call_target="Cholesky" | custom-call | tf_op jit(solution)/shard_map/jit(cholesky)/cholesky | solution.py:49
  1103.3 67.9 %collective-permute-done.4 = f32[512,512]{0,1:T(8,128)} collective-permute-done((f32[512,512]{0,1:T(8,128)}, f32[512,512]{0,1:T(8,128)}, u32[]{:S(2)}, u32[]{:S(2)}) %collective-permute-start.4) | collective-permute-done | bytes 1048608 | tf_op jit(solution)/shard_map/ppermute | solution.py:17
  1203.8 23.6 %custom-call.104 = f32[2,128,128]{2,1,0:T(8,128)S(1)} custom-call(f32[2,128,128]{2,1,0:T(8,128)S(1)} %cholesky.1068), custom_call_target="Cholesky" | custom-call | tf_op jit(solution)/shard_map/jit(cholesky)/cholesky | solution.py:49
  1251.8 23.5 %custom-call.106 = f32[2,128,128]{2,1,0:T(8,128)S(1)} custom-call(f32[2,128,128]{2,1,0:T(8,128)S(1)} %cholesky.1072), custom_call_target="Cholesky" | custom-call | tf_op jit(solution)/shard_map/jit(cholesky)/cholesky | solution.py:49
  1343.1 23.7 %custom-call.110 = f32[2,128,128]{2,1,0:T(8,128)S(1)} custom-call(f32[2,128,128]{2,1,0:T(8,128)S(1)} %convolution_subtract_fusion.11), custom_call_target="Cholesky" | custom-call | tf_op jit(solution)/shard_map/jit(cholesky)/cholesky | solution.py:49
  (230 shorter events, 591.7 us)
Async XLA Ops:
  39.7 29.3 %all-to-all-start.1 = ((bf16[16,128,256]{2,1,0:T(8,128)(2,1)}), bf16[16,128,256]{2,1,0:T(8,128)(2,1)}, u32[]{:S(2)}, u32[]{:S(2)}) async-start(bf16[16,128,256]{2,1,0:T(8,128)(2,1)} %param.12), calls=%async_computation.1 | async-start | bytes 2097152 | tf_op jit(solution)/shard_map/all_to_all | solution.py:55
  43.9 1.4 copy-start.24
  43.9 1326.3 %all-gather.2.cloned.1.call-start = ((), (), s32[]{:S(2)}) async-start(), calls=%async_computation.2 | async-start | bytes 1179648 | tf_op jit(solution)/shard_map/all_gather | solution.py:79
  46.7 367.7 %copy-start.16 = (pred[128,128]{1,0:T(8,128)(4,1)}, pred[128,128]{1,0:T(8,128)(4,1)S(1)}, u32[]{:S(2)}) copy-start(pred[128,128]{1,0:T(8,128)(4,1)S(1)} %iota_compare_fusion.3) | copy-start | bytes 49156
  69.0 1.5 copy-start.5
  69.0 1.9 copy-start.15
  86.8 1.9 copy-start
  180.2 2.5 copy-start.6
  183.4 89.0 %copy-start.7 = (f32[4,384,128]{2,1,0:T(8,128)S(1)}, f32[4,384,128]{2,1,0:T(8,128)}, u32[]{:S(2)}) copy-start(f32[4,384,128]{2,1,0:T(8,128)} %copy-done.6) | copy-start | bytes 2359300
  440.4 1.4 copy-start.2
  622.9 3.5 copy-start.18
  623.1 26.2 %collective-permute-start = (f32[512,512]{0,1:T(8,128)S(1)}, f32[512,512]{0,1:T(8,128)S(1)}, u32[]{:S(2)}, u32[]{:S(2)}) collective-permute-start(f32[512,512]{0,1:T(8,128)S(1)} %get-tuple-element.32), channel_id=1, source_target_pairs={{0,1},{1,0},{2,3},{3,2},{4,5},{5,4},{6,7},{7,6},{8,9},{9,8},{10,11... | collective-permute-start | bytes 3145736 | tf_op jit(solution)/shard_map/ppermute | solution.py:17
  624.4 44.8 %collective-permute-start.1 = (f32[512,512]{0,1:T(8,128)S(1)}, f32[512,512]{0,1:T(8,128)S(1)}, u32[]{:S(2)}, u32[]{:S(2)}) collective-permute-start(f32[512,512]{0,1:T(8,128)S(1)} %get-tuple-element.33), channel_id=1, source_target_pairs={{0,1},{1,0},{2,3},{3,2},{4,5},{5,4},{6,7},{7,6},{8,9},{9,8},{10,11... | collective-permute-start | bytes 3145736 | tf_op jit(solution)/shard_map/ppermute | solution.py:17
  676.7 1.4 copy-start.3
  859.2 3.5 copy-start.20
  859.4 26.2 %collective-permute-start.2 = (f32[512,512]{0,1:T(8,128)S(1)}, f32[512,512]{0,1:T(8,128)S(1)}, u32[]{:S(2)}, u32[]{:S(2)}) collective-permute-start(f32[512,512]{0,1:T(8,128)S(1)} %get-tuple-element.30), channel_id=1, source_target_pairs={{0,2},{2,0},{1,3},{3,1},{4,6},{6,4},{5,7},{7,5},{8,10},{10,8},{9,1... | collective-permute-start | bytes 3145736 | tf_op jit(solution)/shard_map/ppermute | solution.py:17
  859.5 45.1 %collective-permute-start.3 = (f32[512,512]{0,1:T(8,128)S(1)}, f32[512,512]{0,1:T(8,128)S(1)}, u32[]{:S(2)}, u32[]{:S(2)}) collective-permute-start(f32[512,512]{0,1:T(8,128)S(1)} %get-tuple-element.31), channel_id=1, source_target_pairs={{0,2},{2,0},{1,3},{3,1},{4,6},{6,4},{5,7},{7,5},{8,10},{10,8},{9,1... | collective-permute-start | bytes 3145736 | tf_op jit(solution)/shard_map/ppermute | solution.py:17
  912.1 1.4 copy-start.4
  1094.6 4.5 copy-start.19
  1096.1 75.1 %collective-permute-start.4 = (f32[512,512]{0,1:T(8,128)}, f32[512,512]{0,1:T(8,128)}, u32[]{:S(2)}, u32[]{:S(2)}) collective-permute-start(f32[512,512]{0,1:T(8,128)} %get-tuple-element.28), channel_id=1, source_target_pairs={{0,4},{4,0},{1,5},{5,1},{2,6},{6,2},{3,7},{7,3},{8,12},{12,8},{9,1... | collective-permute-start | bytes 3145736 | tf_op jit(solution)/shard_map/ppermute | solution.py:17
  1098.8 93.8 %collective-permute-start.5 = (f32[512,512]{0,1:T(8,128)}, f32[512,512]{0,1:T(8,128)}, u32[]{:S(2)}, u32[]{:S(2)}) collective-permute-start(f32[512,512]{0,1:T(8,128)} %get-tuple-element.29), channel_id=1, source_target_pairs={{0,4},{4,0},{1,5},{5,1},{2,6},{6,2},{3,7},{7,3},{8,12},{12,8},{9,1... | collective-permute-start | bytes 3145736 | tf_op jit(solution)/shard_map/ppermute | solution.py:17
  1202.4 1.4 copy-start.1
  1275.3 91.5 %copy-start.17 = (pred[128,128]{1,0:T(8,128)(4,1)S(1)}, pred[128,128]{1,0:T(8,128)(4,1)}, u32[]{:S(2)}) copy-start(pred[128,128]{1,0:T(8,128)(4,1)} %copy-done.16) | copy-start | bytes 49156
  1368.9 3.3 collective-permute-start.6
  (10 other events, 8.5 us)
Sparse Core Ops, SparseCore 0:
  1099.2 116.1 all-gather.1
where the time goes:
time: 1390 us; the launch traced here: 1380 us
  other arithmetic  992 us (71%)
  waiting for transfers between devices  185 us (13%)
  matrix products  93.5 us (7%)
  local copies, waits for them, and re-layouts  50.8 us (4%)
  blocking collectives  33.1 us (2%)
  between operations  14.8 us (1%)
    another operation x49, other arithmetic, merge_pair(): return jnp.swapaxes(jnp.linalg.cholesky(gram_matrix), 1, 2)  489 us
    another operation x15, other arithmetic, both_factors(): factor = jnp.swapaxes(jnp.linalg.cholesky(gram_matrix), 1, 2)  309 us
    another operation x16, other arithmetic, both_factors(): return jnp.swapaxes(jnp.linalg.cholesky(node_gram), 1, 2)  168 us
    ppermute x7, waiting for transfers between devices, partner(): return lax.ppermute(block, axis, route)  165 us
    all_to_all x1, blocking collectives, body(): lax.all_to_all(col_gen, 'col', split_axis=0, concat_axis=1, tiled=True)  33.1 us
  transfers between devices with their start and end apart: 9, of which 7 were waited for; matrix products, arithmetic and copies ran while one was open for 14% of the time, Pallas kernels for 0%

commit v1 on v0

v1 whole, which is shorter than its diff:
```python
import functools

import jax
import jax.numpy as jnp
from jax import lax
from jax.experimental import pallas as pl
from jax.experimental.pallas import tpu as pltpu
from jax.sharding import PartitionSpec as P

HIGH = lax.Precision.HIGHEST
OFFSETS = (0, 8, 12)
B = 128
F32 = jnp.float32
BF16 = jnp.bfloat16


def split2(x):
    hi = x.astype(BF16)
    lo = (x - hi.astype(F32)).astype(BF16)
    return hi, lo


def split3(x):
    hi = x.astype(BF16)
    rest = x - hi.astype(F32)
    mid = rest.astype(BF16)
    lo = (rest - mid.astype(F32)).astype(BF16)
    return hi, mid, lo


def dot_tn(a, b):
    return lax.dot_general(a, b, (((0,), (0,)), ((), ())), preferred_element_type=F32)


def dot_nn(a, b):
    return jnp.dot(a, b, preferred_element_type=F32)


def gram3(x):
    hi, lo = split2(x)
    cross = dot_tn(hi, lo)
    return dot_tn(hi, hi) + cross + dot_tn(lo, hi)


def eliminate(v, w, p, sub):
    cols = [jnp.broadcast_to(v[:, 8 * p + j : 8 * p + j + 1], (8, B)) for j in range(8)]
    diag = cols[0]
    for j in range(8):
        pivot = jnp.broadcast_to(cols[j][j : j + 1, :], (8, B))
        if j:
            diag = jnp.where(sub == j, pivot, diag)
        else:
            diag = pivot
        if j == 7:
            break
        coef = jnp.where(sub > j, cols[j] / pivot, 0.0)
        for k in range(j + 1, 8):
            cols[k] = cols[k] - coef * jnp.broadcast_to(cols[k][j : j + 1, :], (8, B))
        v = v - coef * jnp.broadcast_to(v[j : j + 1, :], (8, B))
        w = w - coef * jnp.broadcast_to(w[j : j + 1, :], (8, B))
    scale = lax.rsqrt(diag)
    return v * scale, w * scale


def diag_factor(blocks):
    sub = lax.broadcasted_iota(jnp.int32, (8, B), 0)
    lane = lax.broadcasted_iota(jnp.int32, (8, B), 1)
    count = len(blocks)
    left = [[blk[8 * g : 8 * g + 8, :] for g in range(16)] for blk in blocks]
    right = [[jnp.where(lane == sub + 8 * g, 1.0, 0.0).astype(F32) for g in range(16)] for _ in blocks]
    for p in range(16):
        for n in range(count):
            v, w = eliminate(left[n][p], right[n][p], p, sub)
            v = jnp.where(lane >= sub + 8 * p, v, 0.0)
            left[n][p], right[n][p] = v, w
            if p == 15:
                continue
            turned = jnp.transpose(v, (1, 0))
            g = p + 1
            for r in range(8):
                coef = jnp.broadcast_to(turned[8 * g : 8 * g + 8, r : r + 1], (8, B))
                left[n][g] = left[n][g] - coef * jnp.broadcast_to(v[r : r + 1, :], (8, B))
                right[n][g] = right[n][g] - coef * jnp.broadcast_to(w[r : r + 1, :], (8, B))
            if p == 14:
                continue
            both = jnp.concatenate([v, w], axis=1)
            hi, mid, lo = split3(both)
            hv, mv, lv = hi[:, :B], mid[:, :B], lo[:, :B]
            lhs = jnp.concatenate([hv, mv, hv, mv, hv, lv], axis=0)
            rhs = jnp.concatenate([hi, hi, mid, mid, lo, hi], axis=0)
            change = dot_tn(lhs, rhs)
            for g in range(p + 2, 16):
                left[n][g] = left[n][g] - change[8 * g : 8 * g + 8, :B]
                right[n][g] = right[n][g] - change[8 * g : 8 * g + 8, B:]
    return [(jnp.concatenate(left[n], axis=0), jnp.concatenate(right[n], axis=0)) for n in range(count)]


def factor(refs, panels):
    width = refs[0].shape[1]

    def step(p, carry):
        start = pl.multiple_of(p * B, B)
        rows = pl.ds(start, B)
        done = diag_factor([ref[rows, rows] for ref in refs])
        col = lax.broadcasted_iota(jnp.int32, (B, width), 1)
        row = lax.broadcasted_iota(jnp.int32, (B, width), 0)
        his, los = [], []
        for ref, (_, inverse) in zip(refs, done):
            hi, lo = split2(ref[rows, :])
            ihi, ilo = split2(inverse)
            panel = dot_nn(ihi, hi) + dot_nn(ihi, lo) + dot_nn(ilo, hi)
            panel = jnp.where(col >= row + start, panel, 0.0)
            ref[rows, :] = panel
        for ref, (upper, _) in zip(refs, done):
            ref[rows, rows] = upper

        def trail(q, c):
            other = pl.ds(pl.multiple_of(q * B, B), B)
            for ref in refs:
                hi, lo = split2(ref[rows, :])
                qhi, qlo = split2(ref[rows, other])
                ref[other, :] = ref[other, :] - (dot_tn(qhi, hi) + dot_tn(qhi, lo) + dot_tn(qlo, hi))
            return c

        lax.fori_loop(p + 1, width // B, trail, 0)
        return carry

    lax.fori_loop(0, panels, step, 0)


def eye(width):
    return jnp.where(
        lax.broadcasted_iota(jnp.int32, (width, width), 0) == lax.broadcasted_iota(jnp.int32, (width, width), 1), 1.0, 0.0
    ).astype(F32)


def keep_rows(x, limit):
    return jnp.where(lax.broadcasted_iota(jnp.int32, x.shape, 0) < limit, x, 0.0)


def leaf_kernel(rank_ref, trunc_ref, node_ref, gen_ref, upd_ref, out_ref, *grams):
    leaves = gen_ref.shape[0]
    for i in range(leaves):
        gen = gen_ref[i]
        ids = lax.broadcasted_iota(jnp.int32, gen.shape, 1)
        gen = jnp.where(ids < rank_ref[i], gen.astype(F32), 0.0).astype(BF16)
        whole = jnp.concatenate([gen, upd_ref[i]], axis=1)
        grams[i][...] = dot_tn(whole, whole) + eye(whole.shape[1])
    width = grams[0].shape[0]
    factor(grams[:leaves], width // B)
    total = eye(width)
    for i in range(leaves):
        total = total + gram3(keep_rows(grams[i][...], trunc_ref[i]))
    grams[0][...] = total
    kept = out_ref.shape[0]
    factor(grams[:1], kept // B)
    out_ref[...] = keep_rows(grams[0][:kept, :], node_ref[0])


def merge_kernel(node_ref, own_ref, other_ref, out_ref, gram):
    width = gram.shape[0]
    gram[...] = eye(width) + gram3(own_ref[...]) + gram3(other_ref[...])
    kept = out_ref.shape[0]
    factor([gram], kept // B)
    out_ref[...] = keep_rows(gram[:kept, :], node_ref[0])


SMEM = pl.BlockSpec(memory_space=pltpu.SMEM)
VMEM = pl.BlockSpec(memory_space=pltpu.VMEM)
LIMIT = 56 * 1024 * 1024


def leaf_call(rank, trunc, node, gen, upd, kept):
    width = gen.shape[2] + upd.shape[2]
    return pl.pallas_call(
        leaf_kernel,
        out_shape=jax.ShapeDtypeStruct((kept, width), F32),
        in_specs=[SMEM, SMEM, SMEM, VMEM, VMEM],
        out_specs=VMEM,
        scratch_shapes=[pltpu.VMEM((width, width), F32)] * gen.shape[0],
        compiler_params=pltpu.CompilerParams(vmem_limit_bytes=LIMIT),
    )(rank, trunc, node, gen, upd)


def merge_call(node, own, other, kept):
    width = own.shape[1]
    return pl.pallas_call(
        merge_kernel,
        out_shape=jax.ShapeDtypeStruct((kept, width), F32),
        in_specs=[SMEM, VMEM, VMEM],
        out_specs=VMEM,
        scratch_shapes=[pltpu.VMEM((width, width), F32)],
        compiler_params=pltpu.CompilerParams(vmem_limit_bytes=LIMIT),
    )(node, own, other)


def swap(block, axis, distance):
    count = lax.axis_size(axis)
    return lax.ppermute(block, axis, [(i, i ^ distance) for i in range(count)])


def body(row_gen, row_upd, col_gen, col_upd, leaf_rank, leaf_trunc, node_trunc, coupling):
    width = row_gen.shape[2] + row_upd.shape[2]
    kept = 384
    columns = lax.axis_size("col")
    col_gen_full = lax.all_to_all(col_gen, "col", split_axis=0, concat_axis=1, tiled=True)
    col_upd_full = lax.all_to_all(col_upd, "col", split_axis=0, concat_axis=1, tiled=True)
    blocks = [[8 * i + j for j in range(8)] for i in range(columns // 8)]
    mine = lax.all_gather(coupling, "col", axis=0, tiled=True, axis_index_groups=blocks)
    row_pos = lax.axis_index("row")
    col_pos = lax.axis_index("col")
    top = row_pos * (columns // 8) + col_pos // 8
    member = col_pos % 8
    odd = member % 2 == 1
    limits = [node_trunc[top, OFFSETS[h] + (member >> h)][None] for h in range(3)]
    row_factor = leaf_call(leaf_rank, leaf_trunc, limits[0], row_gen, row_upd, kept)
    col_factor = leaf_call(leaf_rank, leaf_trunc, limits[0], col_gen_full, col_upd_full, kept)
    own = jnp.where(odd, col_factor, row_factor)
    other = swap(jnp.where(odd, row_factor, col_factor), "col", 1)
    own = merge_call(limits[1], own, other, kept)
    other = swap(own, "col", 2)
    own = merge_call(limits[2], own, other, kept)
    other = swap(own, "col", 4)
    full = jnp.full((1,), width, jnp.int32)
    top_factor = merge_call(full, own, other, width)
    partner = swap(top_factor, "row", 1)
    share = width // 4
    part = lax.dynamic_slice_in_dim(top_factor, member // 2 * share, share, 0)
    half = swap(jnp.dot(part, mine, precision=HIGH), "col", 1)
    result = lax.dot_general(half, partner, (((1,), (1,)), ((), ())), precision=HIGH)
    result = result / (8 * row_gen.shape[0] * row_gen.shape[1])
    back = swap(result[: share // 2], "col", 1)
    return jnp.where(odd, result[share // 2 :], back)


def solution(mesh):
    return jax.shard_map(
        body,
        mesh=mesh,
        in_specs=(
            P(("row", "col"), None, None),
            P(("row", "col"), None, None),
            P("row", "col", None),
            P("row", "col", None),
            P(("row", "col")),
            P(("row", "col")),
            P(),
            P(("row", "col"), None),
        ),
        out_specs=P(("row", "col"), None),
        check_vma=False,
    )
```

time: 1390 us -> 342 us (0.25)
  other arithmetic: 992 us -> 2.85 us
  Pallas kernels: 0 us -> 192 us
  waiting for transfers between devices: 185 us -> 77.6 us
  matrix products: 93.5 us -> 3.2 us
  local copies, waits for them, and re-layouts: 50.8 us -> 6.07 us
    another operation x80 -> x0, other arithmetic: 966 us -> none  [the longest x49 489 us: merge_pair(): return jnp.swapaxes(jnp.linalg.cholesky(gram_matrix), 1, 2)]
    pallas_call x0 -> x5, Pallas kernels: none -> 192 us  [the longest x2 115 us: leaf_call(): pl.pallas_call(leaf_kernel, out_shape=jax.ShapeDtypeStruct((kept, width),...]
    ppermute x7 -> x6, waiting for transfers between devices: 165 us -> 77.6 us  [swap(): return lax.ppermute(block, axis, [(i, i ^ distance) for i in range(count)])]
    another operation x30 -> x0, matrix products: 48.9 us -> none  [the longest x18 26.8 us: merge_pair(): return jnp.swapaxes(jnp.linalg.cholesky(gram_matrix), 1, 2)]
    dot_general x10 -> x2, matrix products: 44.6 us -> 3.2 us  [the longest x1 2.02 us: body(): half = swap(jnp.dot(part, mine, precision=HIGH), 'col', 1)]
    all_to_all x1, waiting for transfers between devices: 19.7 us -> 0.01 us  [body(): lax.all_to_all(col_upd, 'col', split_axis=0, concat_axis=1, tiled=True)]
  transfers between devices with their start and end apart: 9 -> 8, of which waited for: 7 -> 5; matrix products, arithmetic and copies ran while one was open for 14% -> 1% of each run, Pallas kernels for 0% -> 32%
where the time goes in v1:
time: 342 us; the launch traced here: 341 us
  Pallas kernels  192 us (56%)
  waiting for transfers between devices  77.6 us (23%)
  blocking collectives  33 us (10%)
  between operations  13.5 us (4%)
  starting transfers between devices  12.8 us (4%)
  local copies, waits for them, and re-layouts  6.07 us (2%)
    pallas_call x2, Pallas kernels, leaf_call(): pl.pallas_call(leaf_kernel, out_shape=jax.ShapeDtypeStruct((kept, width),...  115 us
    ppermute x6, waiting for transfers between devices, swap(): return lax.ppermute(block, axis, [(i, i ^ distance) for i in range(count)])  77.6 us
    pallas_call x3, Pallas kernels, merge_call(): pl.pallas_call(merge_kernel, out_shape=jax.ShapeDtypeStruct((kept, width)...  76.7 us
    all_to_all x1, blocking collectives, body(): lax.all_to_all(col_gen, 'col', split_axis=0, concat_axis=1, tiled=True)  33 us
    ppermute x6, starting transfers between devices, swap(): return lax.ppermute(block, axis, [(i, i ^ distance) for i in range(count)])  9.2 us
  transfers between devices with their start and end apart: 8, of which 5 were waited for; matrix products, arithmetic and copies ran while one was open for 1% of the time, Pallas kernels for 32%

profile of v1, /device:TPU:0, one launch (start us, length us, event | category | flops | bytes accessed | tf_op | source)
XLA Modules:
  0.0 341.1 jit_solution(5805916748207762089)
XLA Ops:
  6.5 33.0 %all_to_all.36 = bf16[16,128,256]{2,1,0:T(8,128)(2,1)S(1)} all-to-all(bf16[16,128,256]{2,1,0:T(8,128)(2,1)} %param.10), channel_id=1, replica_groups=mesh['row'=4,'col'=8] {'col'}, dimensions={0} | all-to-all | bytes 2097152 | tf_op jit(solution)/shard_map/all_to_all | solution.py:206
  39.6 3.6 %all-to-all-start.1 = ((bf16[16,128,256]{2,1,0:T(8,128)(2,1)}), bf16[16,128,256]{2,1,0:T(8,128)(2,1)S(1)}, u32[]{:S(2)}, u32[]{:S(2)}) async-start(bf16[16,128,256]{2,1,0:T(8,128)(2,1)} %param.11), calls=%async_computation.1 | async-start | bytes 2097152 | tf_op jit(solution)/shard_map/all_to_all | solution.py:207
  44.5 57.6 %shard_map.83 = f32[384,512]{1,0:T(8,128)} custom-call(s32[2]{0:T(128)} %rank_ref.3, s32[2]{0:T(128)} %trunc_ref.3, s32[1]{0:T(128)} %bitcast.2.node_ref, bf16[2,1024,256]{2,1,0:T(8,128)(2,1)} %gen_ref.1, bf16[2,1024,256]{2,1,0:T(8,128)(2,1)} %upd_ref.1), custom_call_target="tpu_custom_call" | custom-call | tf_op jit(solution)/shard_map/pallas_call | solution.py:175
  102.1 1.1 copy.9
  103.2 1.1 copy.10
  104.3 57.8 %shard_map.82 = f32[384,512]{1,0:T(8,128)} custom-call(s32[2]{0:T(128)} %rank_ref.3, s32[2]{0:T(128)} %trunc_ref.3, s32[1]{0:T(128)} %bitcast.2.node_ref, bf16[2,1024,256]{2,1,0:T(8,128)(2,1)} %bitcast.16, bf16[2,1024,256]{2,1,0:T(8,128)(2,1)} %bitcast.17), custom_call_target="tpu_custom_call" | custom-call | tf_op jit(solution)/shard_map/pallas_call | solution.py:175
  162.1 2.2 broadcast_select_fusion
  164.2 1.9 collective-permute-start
  166.2 16.7 %collective-permute-done.other_ref = f32[384,512]{1,0:T(8,128)S(1)} collective-permute-done((f32[384,512]{1,0:T(8,128)S(1)}, f32[384,512]{1,0:T(8,128)S(1)}, u32[]{:S(2)}, u32[]{:S(2)}) %collective-permute-start) | collective-permute-done | bytes 786464 | tf_op jit(solution)/shard_map/ppermute | solution.py:199
  182.9 0.9 copy-done.2
  183.8 24.0 %shard_map.84.own_ref = f32[384,512]{1,0:T(8,128)} custom-call(s32[1]{0:T(128)} %bitcast.1.node_ref, f32[384,512]{1,0:T(8,128)} %get-tuple-element.6.own_ref, f32[384,512]{1,0:T(8,128)} %copy-done.2), custom_call_target="tpu_custom_call" | custom-call | tf_op jit(solution)/shard_map/pallas_call | solution.py:187
  207.8 1.6 collective-permute-start.1
  209.4 20.1 %collective-permute-done.1.other_ref = f32[384,512]{1,0:T(8,128)S(1)} collective-permute-done((f32[384,512]{1,0:T(8,128)}, f32[384,512]{1,0:T(8,128)S(1)}, u32[]{:S(2)}, u32[]{:S(2)}) %collective-permute-start.1) | collective-permute-done | bytes 786464 | tf_op jit(solution)/shard_map/ppermute | solution.py:199
  229.5 0.9 copy-done.1
  230.4 23.7 %shard_map.85.own_ref = f32[384,512]{1,0:T(8,128)} custom-call(s32[1]{0:T(128)} %bitcast.node_ref, f32[384,512]{1,0:T(8,128)} %shard_map.84.own_ref, f32[384,512]{1,0:T(8,128)} %copy-done.1), custom_call_target="tpu_custom_call" | custom-call | tf_op jit(solution)/shard_map/pallas_call | solution.py:187
  254.1 2.6 collective-permute-start.2
  256.7 29.8 %collective-permute-done.2.other_ref = f32[384,512]{1,0:T(8,128)S(1)} collective-permute-done((f32[384,512]{1,0:T(8,128)}, f32[384,512]{1,0:T(8,128)S(1)}, u32[]{:S(2)}, u32[]{:S(2)}) %collective-permute-start.2) | collective-permute-done | bytes 786464 | tf_op jit(solution)/shard_map/ppermute | solution.py:199
  287.4 29.0 %shard_map.86 = f32[512,512]{1,0:T(8,128)} custom-call(s32[1]{0:T(128)} %constant.60.clone.1.node_ref, f32[384,512]{1,0:T(8,128)} %shard_map.85.own_ref, f32[384,512]{1,0:T(8,128)} %copy-done.3), custom_call_target="tpu_custom_call" | custom-call | tf_op jit(solution)/shard_map/pallas_call | solution.py:187
  316.4 2.0 fusion
  318.4 1.5 collective-permute-start.3
  319.9 7.3 %collective-permute-done.3 = f32[128,512]{1,0:T(8,128)S(1)} collective-permute-done((f32[128,512]{1,0:T(8,128)S(1)}, f32[128,512]{1,0:T(8,128)S(1)}, u32[]{:S(2)}, u32[]{:S(2)}) %collective-permute-start.3) | collective-permute-done | bytes 262176 | tf_op jit(solution)/shard_map/ppermute | solution.py:199
  327.2 1.2 convolution_multiply_fusion
  328.4 1.5 collective-permute-start.5
  329.9 3.7 %collective-permute-done.5 = f32[64,512]{1,0:T(8,128)S(1)} collective-permute-done((f32[64,512]{1,0:T(8,128)S(1)}, f32[64,512]{1,0:T(8,128)S(1)}, u32[]{:S(2)}, u32[]{:S(2)}) %collective-permute-start.5) | collective-permute-done | bytes 131104 | tf_op jit(solution)/shard_map/ppermute | solution.py:199
  (17 shorter events, 2.9 us)
Async XLA Ops:
  39.6 63.6 %all-to-all-start.1 = ((bf16[16,128,256]{2,1,0:T(8,128)(2,1)}), bf16[16,128,256]{2,1,0:T(8,128)(2,1)S(1)}, u32[]{:S(2)}, u32[]{:S(2)}) async-start(bf16[16,128,256]{2,1,0:T(8,128)(2,1)} %param.11), calls=%async_computation.1 | async-start | bytes 2097152 | tf_op jit(solution)/shard_map/all_to_all | solution.py:207
  43.1 273.2 %all-gather.2.cloned.1.call-start = ((), (), s32[]{:S(2)}) async-start(), calls=%async_computation.2 | async-start | bytes 1179648 | tf_op jit(solution)/shard_map/all_gather | solution.py:209
  43.2 0.7 copy-start.4
  104.3 57.8 %copy-start = (f32[384,512]{1,0:T(8,128)S(1)}, f32[384,512]{1,0:T(8,128)}, u32[]{:S(2)}) copy-start(f32[384,512]{1,0:T(8,128)} %shard_map.83) | copy-start | bytes 2359300
  164.2 18.6 %collective-permute-start = (f32[384,512]{1,0:T(8,128)S(1)}, f32[384,512]{1,0:T(8,128)S(1)}, u32[]{:S(2)}, u32[]{:S(2)}) collective-permute-start(f32[384,512]{1,0:T(8,128)S(1)} %get-tuple-element.5), channel_id=1, source_target_pairs={{0,1},{1,0},{2,3},{3,2},{4,5},{5,4},{6,7},{7,6},{8,9},{9,8},{10,11... | collective-permute-start | bytes 2359304 | tf_op jit(solution)/shard_map/ppermute | solution.py:199
  182.9 0.9 copy-start.2
  207.8 21.8 %collective-permute-start.1 = (f32[384,512]{1,0:T(8,128)}, f32[384,512]{1,0:T(8,128)S(1)}, u32[]{:S(2)}, u32[]{:S(2)}) collective-permute-start(f32[384,512]{1,0:T(8,128)} %shard_map.84.own_ref), channel_id=1, source_target_pairs={{0,2},{1,3},{2,0},{3,1},{4,6},{5,7},{6,4},{7,5},{8,10},{9,11},{10,... | collective-permute-start | bytes 2359304 | tf_op jit(solution)/shard_map/ppermute | solution.py:199
  229.5 0.9 copy-start.1
  254.1 32.4 %collective-permute-start.2 = (f32[384,512]{1,0:T(8,128)}, f32[384,512]{1,0:T(8,128)S(1)}, u32[]{:S(2)}, u32[]{:S(2)}) collective-permute-start(f32[384,512]{1,0:T(8,128)} %shard_map.85.own_ref), channel_id=1, source_target_pairs={{0,4},{1,5},{2,6},{3,7},{4,0},{5,1},{6,2},{7,3},{8,12},{9,13},{10,... | collective-permute-start | bytes 2359304 | tf_op jit(solution)/shard_map/ppermute | solution.py:199
  286.5 0.9 copy-start.3
  316.4 10.8 %collective-permute-start.4 = (f32[512,512]{1,0:T(8,128)}, f32[512,512]{1,0:T(8,128)S(1)}, u32[]{:S(2)}, u32[]{:S(2)}) collective-permute-start(f32[512,512]{1,0:T(8,128)} %shard_map.86), channel_id=1, source_target_pairs={{0,8},{8,0},{16,24},{24,16},{1,9},{9,1},{17,25},{25,17},{2,10},{10... | collective-permute-start | bytes 3145736 | tf_op jit(solution)/shard_map/ppermute | solution.py:199
  318.4 8.8 %collective-permute-start.3 = (f32[128,512]{1,0:T(8,128)S(1)}, f32[128,512]{1,0:T(8,128)S(1)}, u32[]{:S(2)}, u32[]{:S(2)}) collective-permute-start(f32[128,512]{1,0:T(8,128)S(1)} %fusion), channel_id=1, source_target_pairs={{0,1},{1,0},{2,3},{3,2},{4,5},{5,4},{6,7},{7,6},{8,9},{9,8},{10,11... | collective-permute-start | bytes 786440 | tf_op jit(solution)/shard_map/ppermute | solution.py:199
  328.4 5.2 %collective-permute-start.5 = (f32[64,512]{1,0:T(8,128)S(1)}, f32[64,512]{1,0:T(8,128)S(1)}, u32[]{:S(2)}, u32[]{:S(2)}) collective-permute-start(f32[64,512]{1,0:T(8,128)S(1)} %slice.9), channel_id=1, source_target_pairs={{0,1},{1,0},{2,3},{3,2},{4,5},{5,4},{6,7},{7,6},{8,9},{9,8},{10,11... | collective-permute-start | bytes 393224 | tf_op jit(solution)/shard_map/ppermute | solution.py:199
Sparse Core Ops, SparseCore 0:
  209.5 41.4 all-gather.1

commit v2 on v1

--- a/solution.py
+++ b/solution.py
@@ -42,57 +42,88 @@
     return dot_tn(hi, hi) + cross + dot_tn(lo, hi)
 
 
-def eliminate(v, w, p, sub):
-    cols = [jnp.broadcast_to(v[:, 8 * p + j : 8 * p + j + 1], (8, B)) for j in range(8)]
-    diag = cols[0]
-    for j in range(8):
-        pivot = jnp.broadcast_to(cols[j][j : j + 1, :], (8, B))
-        if j:
-            diag = jnp.where(sub == j, pivot, diag)
-        else:
-            diag = pivot
-        if j == 7:
-            break
-        coef = jnp.where(sub > j, cols[j] / pivot, 0.0)
-        for k in range(j + 1, 8):
-            cols[k] = cols[k] - coef * jnp.broadcast_to(cols[k][j : j + 1, :], (8, B))
-        v = v - coef * jnp.broadcast_to(v[j : j + 1, :], (8, B))
-        w = w - coef * jnp.broadcast_to(w[j : j + 1, :], (8, B))
-    scale = lax.rsqrt(diag)
-    return v * scale, w * scale
+def recip(x):
+    r = pltpu.reciprocal(x, approx=True)
+    return r * (2.0 - x * r)
+
+
+def sub_row(x, j):
+    return jnp.broadcast_to(x[j : j + 1, :], (8, B))
+
+
+def lane_col(x, k):
+    return jnp.broadcast_to(x[:, k : k + 1], (8, B))
 
 
 def diag_factor(blocks):
     sub = lax.broadcasted_iota(jnp.int32, (8, B), 0)
     lane = lax.broadcasted_iota(jnp.int32, (8, B), 1)
-    count = len(blocks)
+    every = range(len(blocks))
+    G = 4 if len(blocks) == 1 else 2
     left = [[blk[8 * g : 8 * g + 8, :] for g in range(16)] for blk in blocks]
     right = [[jnp.where(lane == sub + 8 * g, 1.0, 0.0).astype(F32) for g in range(16)] for _ in blocks]
-    for p in range(16):
-        for n in range(count):
-            v, w = eliminate(left[n][p], right[n][p], p, sub)
-            v = jnp.where(lane >= sub + 8 * p, v, 0.0)
-            left[n][p], right[n][p] = v, w
-            if p == 15:
+    count = 8 * G
+    for p in range(0, 16, G):
+        vs = [left[m][p : p + G] for m in every]
+        ws = [right[m][p : p + G] for m in every]
+        cols = [[[lane_col(vs[m][a], 8 * p + k) for k in range(8 * (a + 1))] for a in range(G)] for m in every]
+        diag = [[None] * G for _ in every]
+        for j in range(0, count, 2):
+            ja, js = divmod(j, 8)
+            for m in every:
+                col, v, w = cols[m], vs[m], ws[m]
+                d00 = sub_row(col[ja][j], js)
+                d01 = sub_row(col[ja][j], js + 1)
+                d11 = sub_row(col[ja][j + 1], js + 1)
+                det = d00 * d11 - d01 * d01
+                r0 = recip(d00)
+                second = det * r0
+                old = second if js == 0 else jnp.where(sub == js + 1, second, diag[m][ja])
+                diag[m][ja] = jnp.where(sub == js, d00, old)
+                inner = jnp.where(sub == js + 1, d01 * r0, 0.0)
+                v0, v1 = sub_row(v[ja], js), sub_row(v[ja], js + 1)
+                w0, w1 = sub_row(w[ja], js), sub_row(w[ja], js + 1)
+                if js == 6:
+                    v[ja] = v[ja] - inner * v0
+                    w[ja] = w[ja] - inner * w0
+                if j + 2 == count:
+                    continue
+                rdet = recip(det)
+                for a in range(ja, G):
+                    if a == ja and js == 6:
+                        continue
+                    x, y = col[a][j], col[a][j + 1]
+                    px = (d11 * x - d01 * y) * rdet
+                    py = (d00 * y - d01 * x) * rdet
+                    if a == ja:
+                        px = jnp.where(sub > js + 1, px, 0.0)
+                        py = jnp.where(sub > js + 1, py, 0.0)
+                    for k in range(j + 2, 8 * (a + 1)):
+                        ka, ks = divmod(k, 8)
+                        col[a][k] = col[a][k] - (px * sub_row(col[ka][j], ks) + py * sub_row(col[ka][j + 1], ks))
+                    if a == ja:
+                        px = px + inner
+                    v[a] = v[a] - (px * v0 + py * v1)
+                    w[a] = w[a] - (px * w0 + py * w1)
+        for m in every:
+            v, w = vs[m], ws[m]
+            for a in range(G):
+                scale = lax.rsqrt(diag[m][a])
+                v[a] = jnp.where(lane >= sub + 8 * (p + a), v[a] * scale, 0.0)
+                w[a] = w[a] * scale
+                left[m][p + a], right[m][p + a] = v[a], w[a]
+            if p + G == 16:
                 continue
-            turned = jnp.transpose(v, (1, 0))
-            g = p + 1
-            for r in range(8):
-                coef = jnp.broadcast_to(turned[8 * g : 8 * g + 8, r : r + 1], (8, B))
-                left[n][g] = left[n][g] - coef * jnp.broadcast_to(v[r : r + 1, :], (8, B))
-                right[n][g] = right[n][g] - coef * jnp.broadcast_to(w[r : r + 1, :], (8, B))
-            if p == 14:
-                continue
-            both = jnp.concatenate([v, w], axis=1)
+            both = jnp.concatenate([jnp.concatenate(v, axis=0), jnp.concatenate(w, axis=0)], axis=1)
             hi, mid, lo = split3(both)
             hv, mv, lv = hi[:, :B], mid[:, :B], lo[:, :B]
             lhs = jnp.concatenate([hv, mv, hv, mv, hv, lv], axis=0)
             rhs = jnp.concatenate([hi, hi, mid, mid, lo, hi], axis=0)
             change = dot_tn(lhs, rhs)
-            for g in range(p + 2, 16):
-                left[n][g] = left[n][g] - change[8 * g : 8 * g + 8, :B]
-                right[n][g] = right[n][g] - change[8 * g : 8 * g + 8, B:]
-    return [(jnp.concatenate(left[n], axis=0), jnp.concatenate(right[n], axis=0)) for n in range(count)]
+            for g in range(p + G, 16):
+                left[m][g] = left[m][g] - change[8 * g : 8 * g + 8, :B]
+                right[m][g] = right[m][g] - change[8 * g : 8 * g + 8, B:]
+    return [(jnp.concatenate(left[m], axis=0), jnp.concatenate(right[m], axis=0)) for m in every]
 
 
 def factor(refs, panels):
@@ -179,6 +210,7 @@
         out_specs=VMEM,
         scratch_shapes=[pltpu.VMEM((width, width), F32)] * gen.shape[0],
         compiler_params=pltpu.CompilerParams(vmem_limit_bytes=LIMIT),
+        cost_estimate=pl.CostEstimate(flops=50_000_000_000, bytes_accessed=100_000_000, transcendentals=0),
     )(rank, trunc, node, gen, upd)
 
 
@@ -203,8 +235,9 @@
     width = row_gen.shape[2] + row_upd.shape[2]
     kept = 384
     columns = lax.axis_size("col")
-    col_gen_full = lax.all_to_all(col_gen, "col", split_axis=0, concat_axis=1, tiled=True)
-    col_upd_full = lax.all_to_all(col_upd, "col", split_axis=0, concat_axis=1, tiled=True)
+    col_both = jnp.concatenate([col_gen, col_upd], axis=2)
+    col_full = lax.all_to_all(col_both, "col", split_axis=0, concat_axis=1, tiled=True)
+    cut = col_gen.shape[2]
     blocks = [[8 * i + j for j in range(8)] for i in range(columns // 8)]
     mine = lax.all_gather(coupling, "col", axis=0, tiled=True, axis_index_groups=blocks)
     row_pos = lax.axis_index("row")
@@ -214,7 +247,7 @@
     odd = member % 2 == 1
     limits = [node_trunc[top, OFFSETS[h] + (member >> h)][None] for h in range(3)]
     row_factor = leaf_call(leaf_rank, leaf_trunc, limits[0], row_gen, row_upd, kept)
-    col_factor = leaf_call(leaf_rank, leaf_trunc, limits[0], col_gen_full, col_upd_full, kept)
+    col_factor = leaf_call(leaf_rank, leaf_trunc, limits[0], col_full[:, :, :cut], col_full[:, :, cut:], kept)
     own = jnp.where(odd, col_factor, row_factor)
     other = swap(jnp.where(odd, row_factor, col_factor), "col", 1)
     own = merge_call(limits[1], own, other, kept)

time: 342 us -> 266 us (0.78)
  Pallas kernels: 192 us -> 131 us
  blocking collectives: 33 us -> 0 us
  waiting for transfers between devices: 77.6 us -> 93.1 us
    pallas_call x2, Pallas kernels: 115 us -> 77.7 us  [leaf_call(): pl.pallas_call(leaf_kernel, out_shape=jax.ShapeDtypeStruct((kept, width),...]
    all_to_all x1 -> x0, blocking collectives: 33 us -> none  [body(): lax.all_to_all(col_gen, 'col', split_axis=0, concat_axis=1, tiled=True)]
    pallas_call x3, Pallas kernels: 76.7 us -> 53.3 us  [merge_call(): pl.pallas_call(merge_kernel, out_shape=jax.ShapeDtypeStruct((kept, width)...]
    all_to_all x1, waiting for transfers between devices: 0.01 us -> 8.78 us  [body(): lax.all_to_all(col_both, 'col', split_axis=0, concat_axis=1, tiled=True)]
    ppermute x6, waiting for transfers between devices: 77.6 us -> 84.3 us  [swap(): return lax.ppermute(block, axis, [(i, i ^ distance) for i in range(count)])]
    all_to_all x1, starting transfers between devices: 3.59 us -> 7.38 us  [body(): lax.all_to_all(col_both, 'col', split_axis=0, concat_axis=1, tiled=True)]
  transfers between devices with their start and end apart: 8 -> 8, of which waited for: 5 -> 6; matrix products, arithmetic and copies ran while one was open for 1% -> 1% of each run, Pallas kernels for 32% -> 28%
where the time goes in v2:
time: 266 us
  Pallas kernels  131 us (49%)
  waiting for transfers between devices  93.1 us (35%)
  starting transfers between devices  14 us (5%)
  between operations  13.5 us (5%)
  other arithmetic  5.91 us (2%)
  local copies, waits for them, and re-layouts  4.96 us (2%)
  matrix products  3.2 us (1%)
    ppermute x6, waiting for transfers between devices, swap(): return lax.ppermute(block, axis, [(i, i ^ distance) for i in range(count)])  84.3 us
    pallas_call x2, Pallas kernels, leaf_call(): pl.pallas_call(leaf_kernel, out_shape=jax.ShapeDtypeStruct((kept, width),...  77.7 us
    pallas_call x3, Pallas kernels, merge_call(): pl.pallas_call(merge_kernel, out_shape=jax.ShapeDtypeStruct((kept, width)...  53.3 us
    all_to_all x1, waiting for transfers between devices, body(): lax.all_to_all(col_both, 'col', split_axis=0, concat_axis=1, tiled=True)  8.78 us
    all_to_all x1, starting transfers between devices, body(): lax.all_to_all(col_both, 'col', split_axis=0, concat_axis=1, tiled=True)  7.38 us
    ppermute x6, starting transfers between devices, swap(): return lax.ppermute(block, axis, [(i, i ^ distance) for i in range(count)])  6.59 us
  transfers between devices with their start and end apart: 8, of which 6 were waited for; matrix products, arithmetic and copies ran while one was open for 1% of the time, Pallas kernels for 28%

profile of v2, /device:TPU:0, one launch (start us, length us, event | category | flops | bytes accessed | tf_op | source)
XLA Modules:
  0.0 265.6 jit_solution(657809311465446042)
XLA Ops:
  6.5 3.1 %pad_maximum_fusion = bf16[16,128,512]{2,1,0:T(8,128)(2,1)} fusion(bf16[16,128,256]{2,1,0:T(8,128)(2,1)} %param.11, bf16[16,128,256]{2,1,0:T(8,128)(2,1)} %param.10), kind=kLoop, calls=%fused_computation | loop fusion | flops 4194304 | bytes 4194304 | tf_op jit(solution)/shard_map/concatenate | solution.py:238
  9.6 7.4 %all-to-all-start = ((bf16[16,128,512]{2,1,0:T(8,128)(2,1)}), bf16[16,128,512]{2,1,0:T(8,128)(2,1)S(1)}, u32[]{:S(2)}, u32[]{:S(2)}) async-start(bf16[16,128,512]{2,1,0:T(8,128)(2,1)} %pad_maximum_fusion), calls=%async_computation | async-start | bytes 4194304 | tf_op jit(solution)/shard_map/all_to_all | solution.py:239
  17.7 38.7 %shard_map.83 = f32[384,512]{1,0:T(8,128)} custom-call(s32[2]{0:T(128)} %rank_ref.3, s32[2]{0:T(128)} %trunc_ref.3, s32[1]{0:T(128)} %bitcast.2.node_ref, bf16[2,1024,256]{2,1,0:T(8,128)(2,1)} %gen_ref.1, bf16[2,1024,256]{2,1,0:T(8,128)(2,1)} %upd_ref.1), custom_call_target="tpu_custom_call" | custom-call | flops 49999998976 | bytes 100000000 | tf_op jit(solution)/shard_map/pallas_call | solution.py:206
  56.4 8.8 %all-to-all-done = bf16[16,128,512]{2,1,0:T(8,128)(2,1)S(1)} async-done(((bf16[16,128,512]{2,1,0:T(8,128)(2,1)}), bf16[16,128,512]{2,1,0:T(8,128)(2,1)S(1)}, u32[]{:S(2)}, u32[]{:S(2)}) %all-to-all-start) | async-done | bytes 2097184 | tf_op jit(solution)/shard_map/all_to_all | solution.py:239
  65.4 1.5 fusion.3
  66.9 38.9 %shard_map.82 = f32[384,512]{1,0:T(8,128)} custom-call(s32[2]{0:T(128)} %rank_ref.3, s32[2]{0:T(128)} %trunc_ref.3, s32[1]{0:T(128)} %bitcast.2.node_ref, bf16[2,1024,256]{2,1,0:T(8,128)(2,1)} %get-tuple-element.6.gen_ref, bf16[2,1024,256]{2,1,0:T(8,128)(2,1)} %get-tuple-element.5.upd_ref), custom_call_target="tpu_custom_call" | custom-call | flops 49999998976 | bytes 100000000 | tf_op jit(solution)/shard_map/pallas_call | solution.py:206
  105.9 2.2 broadcast_select_fusion
  108.0 1.5 collective-permute-start
  109.5 16.8 %collective-permute-done.other_ref = f32[384,512]{1,0:T(8,128)S(1)} collective-permute-done((f32[384,512]{1,0:T(8,128)S(1)}, f32[384,512]{1,0:T(8,128)S(1)}, u32[]{:S(2)}, u32[]{:S(2)}) %collective-permute-start) | collective-permute-done | bytes 786464 | tf_op jit(solution)/shard_map/ppermute | solution.py:231
  126.3 0.9 copy-done.1
  127.2 16.9 %shard_map.84.own_ref = f32[384,512]{1,0:T(8,128)} custom-call(s32[1]{0:T(128)} %bitcast.1.node_ref, f32[384,512]{1,0:T(8,128)} %get-tuple-element.8.own_ref, f32[384,512]{1,0:T(8,128)} %copy-done.1), custom_call_target="tpu_custom_call" | custom-call | tf_op jit(solution)/shard_map/pallas_call | solution.py:219
  144.1 0.8 collective-permute-start.1
  144.9 21.1 %collective-permute-done.1.other_ref = f32[384,512]{1,0:T(8,128)S(1)} collective-permute-done((f32[384,512]{1,0:T(8,128)}, f32[384,512]{1,0:T(8,128)S(1)}, u32[]{:S(2)}, u32[]{:S(2)}) %collective-permute-start.1) | collective-permute-done | bytes 786464 | tf_op jit(solution)/shard_map/ppermute | solution.py:231
  166.0 0.9 copy-done
  166.9 16.7 %shard_map.85.own_ref = f32[384,512]{1,0:T(8,128)} custom-call(s32[1]{0:T(128)} %bitcast.node_ref, f32[384,512]{1,0:T(8,128)} %shard_map.84.own_ref, f32[384,512]{1,0:T(8,128)} %copy-done), custom_call_target="tpu_custom_call" | custom-call | tf_op jit(solution)/shard_map/pallas_call | solution.py:219
  183.6 3.4 %collective-permute-start.2 = (f32[384,512]{1,0:T(8,128)}, f32[384,512]{1,0:T(8,128)S(1)}, u32[]{:S(2)}, u32[]{:S(2)}) collective-permute-start(f32[384,512]{1,0:T(8,128)} %shard_map.85.own_ref), channel_id=1, source_target_pairs={{0,4},{1,5},{2,6},{3,7},{4,0},{5,1},{6,2},{7,3},{8,12},{9,13},{10,... | collective-permute-start | bytes 2359304 | tf_op jit(solution)/shard_map/ppermute | solution.py:231
  187.1 33.3 %collective-permute-done.2.other_ref = f32[384,512]{1,0:T(8,128)S(1)} collective-permute-done((f32[384,512]{1,0:T(8,128)}, f32[384,512]{1,0:T(8,128)S(1)}, u32[]{:S(2)}, u32[]{:S(2)}) %collective-permute-start.2) | collective-permute-done | bytes 786464 | tf_op jit(solution)/shard_map/ppermute | solution.py:231
  220.4 0.9 copy-done.2
  221.2 19.6 %shard_map.86 = f32[512,512]{1,0:T(8,128)} custom-call(s32[1]{0:T(128)} %constant.60.clone.1.node_ref, f32[384,512]{1,0:T(8,128)} %shard_map.85.own_ref, f32[384,512]{1,0:T(8,128)} %copy-done.2), custom_call_target="tpu_custom_call" | custom-call | tf_op jit(solution)/shard_map/pallas_call | solution.py:219
  240.9 2.0 fusion
  243.3 8.3 %collective-permute-done.3 = f32[128,512]{1,0:T(8,128)S(1)} collective-permute-done((f32[128,512]{1,0:T(8,128)S(1)}, f32[128,512]{1,0:T(8,128)S(1)}, u32[]{:S(2)}, u32[]{:S(2)}) %collective-permute-start.3) | collective-permute-done | bytes 262176 | tf_op jit(solution)/shard_map/ppermute | solution.py:231
  251.7 1.2 convolution_multiply_fusion
  253.3 4.8 %collective-permute-done.5 = f32[64,512]{1,0:T(8,128)S(1)} collective-permute-done((f32[64,512]{1,0:T(8,128)S(1)}, f32[64,512]{1,0:T(8,128)S(1)}, u32[]{:S(2)}, u32[]{:S(2)}) %collective-permute-start.5) | collective-permute-done | bytes 131104 | tf_op jit(solution)/shard_map/ppermute | solution.py:231
  258.1 0.7 slice_select_fusion
  (17 shorter events, 1.8 us)
Async XLA Ops:
  9.6 7.5 %copy-start.4 = (s32[4,14]{1,0:T(4,128)S(1)}, s32[4,14]{1,0:T(4,128)}, u32[]{:S(2)}) copy-start(s32[4,14]{1,0:T(4,128)} %param.14) | copy-start | bytes 676
  9.6 55.6 %all-to-all-start = ((bf16[16,128,512]{2,1,0:T(8,128)(2,1)}), bf16[16,128,512]{2,1,0:T(8,128)(2,1)S(1)}, u32[]{:S(2)}, u32[]{:S(2)}) async-start(bf16[16,128,512]{2,1,0:T(8,128)(2,1)} %pad_maximum_fusion), calls=%async_computation | async-start | bytes 4194304 | tf_op jit(solution)/shard_map/all_to_all | solution.py:239
  17.0 223.9 %all-gather.2.cloned.1.call-start = ((), (), s32[]{:S(2)}) async-start(), calls=%async_computation.1 | async-start | bytes 1179648 | tf_op jit(solution)/shard_map/all_gather | solution.py:242
  66.9 39.0 %copy-start.3 = (f32[384,512]{1,0:T(8,128)S(1)}, f32[384,512]{1,0:T(8,128)}, u32[]{:S(2)}) copy-start(f32[384,512]{1,0:T(8,128)} %shard_map.83) | copy-start | bytes 2359300
  108.0 18.2 %collective-permute-start = (f32[384,512]{1,0:T(8,128)S(1)}, f32[384,512]{1,0:T(8,128)S(1)}, u32[]{:S(2)}, u32[]{:S(2)}) collective-permute-start(f32[384,512]{1,0:T(8,128)S(1)} %get-tuple-element.7), channel_id=1, source_target_pairs={{0,1},{1,0},{2,3},{3,2},{4,5},{5,4},{6,7},{7,6},{8,9},{9,8},{10,11... | collective-permute-start | bytes 2359304 | tf_op jit(solution)/shard_map/ppermute | solution.py:231
  126.3 0.9 copy-start.1
  144.1 21.9 %collective-permute-start.1 = (f32[384,512]{1,0:T(8,128)}, f32[384,512]{1,0:T(8,128)S(1)}, u32[]{:S(2)}, u32[]{:S(2)}) collective-permute-start(f32[384,512]{1,0:T(8,128)} %shard_map.84.own_ref), channel_id=1, source_target_pairs={{0,2},{1,3},{2,0},{3,1},{4,6},{5,7},{6,4},{7,5},{8,10},{9,11},{10,... | collective-permute-start | bytes 2359304 | tf_op jit(solution)/shard_map/ppermute | solution.py:231
  166.0 0.9 copy-start
  183.6 36.8 %collective-permute-start.2 = (f32[384,512]{1,0:T(8,128)}, f32[384,512]{1,0:T(8,128)S(1)}, u32[]{:S(2)}, u32[]{:S(2)}) collective-permute-start(f32[384,512]{1,0:T(8,128)} %shard_map.85.own_ref), channel_id=1, source_target_pairs={{0,4},{1,5},{2,6},{3,7},{4,0},{5,1},{6,2},{7,3},{8,12},{9,13},{10,... | collective-permute-start | bytes 2359304 | tf_op jit(solution)/shard_map/ppermute | solution.py:231
  220.4 0.9 copy-start.2
  240.9 10.8 %collective-permute-start.4 = (f32[512,512]{1,0:T(8,128)}, f32[512,512]{1,0:T(8,128)S(1)}, u32[]{:S(2)}, u32[]{:S(2)}) collective-permute-start(f32[512,512]{1,0:T(8,128)} %shard_map.86), channel_id=1, source_target_pairs={{0,8},{8,0},{16,24},{24,16},{1,9},{9,1},{17,25},{25,17},{2,10},{10... | collective-permute-start | bytes 3145736 | tf_op jit(solution)/shard_map/ppermute | solution.py:231
  242.9 8.8 %collective-permute-start.3 = (f32[128,512]{1,0:T(8,128)S(1)}, f32[128,512]{1,0:T(8,128)S(1)}, u32[]{:S(2)}, u32[]{:S(2)}) collective-permute-start(f32[128,512]{1,0:T(8,128)S(1)} %fusion), channel_id=1, source_target_pairs={{0,1},{1,0},{2,3},{3,2},{4,5},{5,4},{6,7},{7,6},{8,9},{9,8},{10,11... | collective-permute-start | bytes 786440 | tf_op jit(solution)/shard_map/ppermute | solution.py:231
  252.9 5.2 %collective-permute-start.5 = (f32[64,512]{1,0:T(8,128)S(1)}, f32[64,512]{1,0:T(8,128)S(1)}, u32[]{:S(2)}, u32[]{:S(2)}) collective-permute-start(f32[64,512]{1,0:T(8,128)S(1)} %slice.19), channel_id=1, source_target_pairs={{0,1},{1,0},{2,3},{3,2},{4,5},{5,4},{6,7},{7,6},{8,9},{9,8},{10,11... | collective-permute-start | bytes 393224 | tf_op jit(solution)/shard_map/ppermute | solution.py:231
Sparse Core Ops, SparseCore 0:
  145.0 41.4 all-gather.1

commit v3 on v2

--- a/solution.py
+++ b/solution.py
@@ -126,7 +126,7 @@
     return [(jnp.concatenate(left[m], axis=0), jnp.concatenate(right[m], axis=0)) for m in every]
 
 
-def factor(refs, panels):
+def factor(refs, panels, after=None):
     width = refs[0].shape[1]
 
     def step(p, carry):
@@ -153,6 +153,8 @@
                 ref[other, :] = ref[other, :] - (dot_tn(qhi, hi) + dot_tn(qhi, lo) + dot_tn(qlo, hi))
             return c
 
+        if after is not None:
+            after(p)
         lax.fori_loop(p + 1, width // B, trail, 0)
         return carry
 
@@ -169,7 +171,10 @@
     return jnp.where(lax.broadcasted_iota(jnp.int32, x.shape, 0) < limit, x, 0.0)
 
 
-def leaf_kernel(rank_ref, trunc_ref, node_ref, gen_ref, upd_ref, out_ref, *grams):
+KEPT = 3
+
+
+def leaf_total(rank_ref, trunc_ref, gen_ref, upd_ref, grams):
     leaves = gen_ref.shape[0]
     for i in range(leaves):
         gen = gen_ref[i]
@@ -178,22 +183,102 @@
         whole = jnp.concatenate([gen, upd_ref[i]], axis=1)
         grams[i][...] = dot_tn(whole, whole) + eye(whole.shape[1])
     width = grams[0].shape[0]
-    factor(grams[:leaves], width // B)
+    factor(grams, width // B)
     total = eye(width)
     for i in range(leaves):
         total = total + gram3(keep_rows(grams[i][...], trunc_ref[i]))
     grams[0][...] = total
-    kept = out_ref.shape[0]
-    factor(grams[:1], kept // B)
-    out_ref[...] = keep_rows(grams[0][:kept, :], node_ref[0])
-
-
-def merge_kernel(node_ref, own_ref, other_ref, out_ref, gram):
+
+
+def kept_panel(gram, p, limit):
+    return keep_rows(gram[p * B : (p + 1) * B, p * B :], limit - p * B)
+
+
+def leaf_kernel(rank_ref, trunc_ref, node_ref, gen_ref, upd_ref, *refs):
+    outs, grams = refs[:KEPT], refs[KEPT:]
+    leaf_total(rank_ref, trunc_ref, gen_ref, upd_ref, grams)
+    factor(grams[:1], KEPT)
+    for p in range(KEPT):
+        outs[p][...] = kept_panel(grams[0], p, node_ref[0])
+
+
+def tree_kernel(rank_ref, trunc_ref, node_ref, gen_ref, upd_ref, *refs):
+    rows, out_ref, refs = refs[:KEPT], refs[KEPT], refs[KEPT + 1 :]
+    grams, refs = refs[: gen_ref.shape[0]], refs[gen_ref.shape[0] :]
+    own, send, land = refs[:KEPT], refs[KEPT : 2 * KEPT], refs[2 * KEPT : 3 * KEPT]
+    send_sem, recv_sem = refs[3 * KEPT :]
+    gram = grams[0]
     width = gram.shape[0]
-    gram[...] = eye(width) + gram3(own_ref[...]) + gram3(other_ref[...])
-    kept = out_ref.shape[0]
-    factor([gram], kept // B)
-    out_ref[...] = keep_rows(gram[:kept, :], node_ref[0])
+    place = lax.axis_index("col")
+    odd = place % 2
+    partners = [place + d * (1 - 2 * ((place // d) % 2)) for d in (1, 2, 4)]
+
+    barrier = pltpu.get_barrier_semaphore()
+    for other in partners:
+        pl.semaphore_signal(barrier, inc=1, device_id={"col": other}, device_id_type=pl.DeviceIdType.MESH)
+    pl.semaphore_wait(barrier, 3)
+
+    def copy(h, p):
+        return pltpu.make_async_remote_copy(
+            src_ref=send[p].at[h],
+            dst_ref=land[p].at[h],
+            send_sem=send_sem.at[h, p],
+            recv_sem=recv_sem.at[h, p],
+            device_id={"col": partners[h]},
+            device_id_type=pl.DeviceIdType.MESH,
+        )
+
+    leaf_total(rank_ref, trunc_ref, gen_ref, upd_ref, grams)
+
+    def level(h, carry):
+        def after(p):
+            for c in range(KEPT):
+
+                @pl.when((p == c) & (h == 0))
+                def _(c=c):
+                    mine = kept_panel(gram, c, node_ref[0])
+
+                    @pl.when(odd == 1)
+                    def _():
+                        own[c][...] = mine
+                        send[c][0] = rows[c][...]
+
+                    @pl.when(odd == 0)
+                    def _():
+                        own[c][...] = rows[c][...]
+                        send[c][0] = mine
+
+                    copy(0, c).start()
+
+                for hh in (1, 2):
+
+                    @pl.when((p == c) & (h == hh))
+                    def _(c=c, hh=hh):
+                        mine = kept_panel(gram, c, node_ref[hh])
+                        own[c][...] = mine
+                        send[c][hh] = mine
+                        copy(hh, c).start()
+
+        factor([gram], KEPT + h // 3, after)
+
+        @pl.when(h < 3)
+        def _():
+            gram[...] = eye(width)
+            for p in range(KEPT):
+                gram[p * B :, p * B :] = gram[p * B :, p * B :] + gram3(own[p][...])
+
+        for p in range(KEPT):
+            for hh in range(3):
+
+                @pl.when(h == hh)
+                def _(p=p, hh=hh):
+                    copy(hh, p).wait()
+                    gram[p * B :, p * B :] = gram[p * B :, p * B :] + gram3(land[p][hh])
+
+        return carry
+
+    lax.fori_loop(0, 4, level, 0)
+    out_ref[...] = gram[...]
 
 
 SMEM = pl.BlockSpec(memory_space=pltpu.SMEM)
@@ -201,29 +286,37 @@
 LIMIT = 56 * 1024 * 1024
 
 
-def leaf_call(rank, trunc, node, gen, upd, kept):
+def panel_shapes(width, lead=()):
+    return [lead + (B, width - p * B) for p in range(KEPT)]
+
+
+def leaf_call(rank, trunc, node, gen, upd):
     width = gen.shape[2] + upd.shape[2]
     return pl.pallas_call(
         leaf_kernel,
-        out_shape=jax.ShapeDtypeStruct((kept, width), F32),
+        out_shape=[jax.ShapeDtypeStruct(shape, F32) for shape in panel_shapes(width)],
         in_specs=[SMEM, SMEM, SMEM, VMEM, VMEM],
-        out_specs=VMEM,
+        out_specs=[VMEM] * KEPT,
         scratch_shapes=[pltpu.VMEM((width, width), F32)] * gen.shape[0],
         compiler_params=pltpu.CompilerParams(vmem_limit_bytes=LIMIT),
         cost_estimate=pl.CostEstimate(flops=50_000_000_000, bytes_accessed=100_000_000, transcendentals=0),
     )(rank, trunc, node, gen, upd)
 
 
-def merge_call(node, own, other, kept):
-    width = own.shape[1]
+def tree_call(rank, trunc, node, gen, upd, rows):
+    width = gen.shape[2] + upd.shape[2]
     return pl.pallas_call(
-        merge_kernel,
-        out_shape=jax.ShapeDtypeStruct((kept, width), F32),
-        in_specs=[SMEM, VMEM, VMEM],
+        tree_kernel,
+        out_shape=jax.ShapeDtypeStruct((width, width), F32),
+        in_specs=[SMEM, SMEM, SMEM, VMEM, VMEM] + [VMEM] * KEPT,
         out_specs=VMEM,
-        scratch_shapes=[pltpu.VMEM((width, width), F32)],
-        compiler_params=pltpu.CompilerParams(vmem_limit_bytes=LIMIT),
-    )(node, own, other)
+        scratch_shapes=[pltpu.VMEM((width, width), F32)] * gen.shape[0]
+        + [pltpu.VMEM(shape, F32) for shape in panel_shapes(width)]
+        + [pltpu.VMEM(shape, F32) for shape in panel_shapes(width, (3,))] * 2
+        + [pltpu.SemaphoreType.DMA((3, KEPT)), pltpu.SemaphoreType.DMA((3, KEPT))],
+        compiler_params=pltpu.CompilerParams(vmem_limit_bytes=LIMIT, collective_id=0, has_side_effects=True),
+        cost_estimate=pl.CostEstimate(flops=50_000_000_000, bytes_accessed=100_000_000, transcendentals=0),
+    )(rank, trunc, node, gen, upd, *rows)
 
 
 def swap(block, axis, distance):
@@ -233,7 +326,6 @@
 
 def body(row_gen, row_upd, col_gen, col_upd, leaf_rank, leaf_trunc, node_trunc, coupling):
     width = row_gen.shape[2] + row_upd.shape[2]
-    kept = 384
     columns = lax.axis_size("col")
     col_both = jnp.concatenate([col_gen, col_upd], axis=2)
     col_full = lax.all_to_all(col_both, "col", split_axis=0, concat_axis=1, tiled=True)
@@ -245,17 +337,9 @@
     top = row_pos * (columns // 8) + col_pos // 8
     member = col_pos % 8
     odd = member % 2 == 1
-    limits = [node_trunc[top, OFFSETS[h] + (member >> h)][None] for h in range(3)]
-    row_factor = leaf_call(leaf_rank, leaf_trunc, limits[0], row_gen, row_upd, kept)
-    col_factor = leaf_call(leaf_rank, leaf_trunc, limits[0], col_full[:, :, :cut], col_full[:, :, cut:], kept)
-    own = jnp.where(odd, col_factor, row_factor)
-    other = swap(jnp.where(odd, row_factor, col_factor), "col", 1)
-    own = merge_call(limits[1], own, other, kept)
-    other = swap(own, "col", 2)
-    own = merge_call(limits[2], own, other, kept)
-    other = swap(own, "col", 4)
-    full = jnp.full((1,), width, jnp.int32)
-    top_factor = merge_call(full, own, other, width)
+    limits = jnp.stack([node_trunc[top, OFFSETS[h] + (member >> h)] for h in range(3)])
+    rows = leaf_call(leaf_rank, leaf_trunc, limits, row_gen, row_upd)
+    top_factor = tree_call(leaf_rank, leaf_trunc, limits, col_full[:, :, :cut], col_full[:, :, cut:], rows)
     partner = swap(top_factor, "row", 1)
     share = width // 4
     part = lax.dynamic_slice_in_dim(top_factor, member // 2 * share, share, 0)

time: 266 us -> 212 us (0.80)
  waiting for transfers between devices: 93.1 us -> 28.8 us
  Pallas kernels: 131 us -> 147 us
  starting transfers between devices: 14 us -> 10.9 us
    ppermute x6 -> x3, waiting for transfers between devices: 84.3 us -> 10.5 us  [swap(): return lax.ppermute(block, axis, [(i, i ^ distance) for i in range(count)])]
    pallas_call x5 -> x2, Pallas kernels: 131 us -> 147 us  [the longest x1 109 us: tree_call(): pl.pallas_call(tree_kernel, out_shape=jax.ShapeDtypeStruct((width, width)...]
    all_to_all x1, waiting for transfers between devices: 8.78 us -> 17.6 us  [body(): lax.all_to_all(col_both, 'col', split_axis=0, concat_axis=1, tiled=True)]
    ppermute x6 -> x3, starting transfers between devices: 6.59 us -> 3.45 us  [swap(): return lax.ppermute(block, axis, [(i, i ^ distance) for i in range(count)])]
  transfers between devices with their start and end apart: 8 -> 5, of which waited for: 6 -> 3; matrix products, arithmetic and copies ran while one was open for 1% -> 3% of each run, Pallas kernels for 28% -> 69%
where the time goes in v3:
time: 212 us
  Pallas kernels  147 us (69%)
  waiting for transfers between devices  28.8 us (14%)
  between operations  13.5 us (6%)
  starting transfers between devices  10.9 us (5%)
  other arithmetic  6.29 us (3%)
  matrix products  3.21 us (2%)
  local copies, waits for them, and re-layouts  2.35 us (1%)
    pallas_call x1, Pallas kernels, tree_call(): pl.pallas_call(tree_kernel, out_shape=jax.ShapeDtypeStruct((width, width)...  109 us
    pallas_call x1, Pallas kernels, leaf_call(): pl.pallas_call(leaf_kernel, out_shape=[jax.ShapeDtypeStruct(shape, F32) f...  38 us
    all_to_all x1, waiting for transfers between devices, body(): lax.all_to_all(col_both, 'col', split_axis=0, concat_axis=1, tiled=True)  17.6 us
    ppermute x3, waiting for transfers between devices, swap(): return lax.ppermute(block, axis, [(i, i ^ distance) for i in range(count)])  10.5 us
    all_to_all x1, starting transfers between devices, body(): lax.all_to_all(col_both, 'col', split_axis=0, concat_axis=1, tiled=True)  7.38 us
  transfers between devices with their start and end apart: 5, of which 3 were waited for; matrix products, arithmetic and copies ran while one was open for 3% of the time, Pallas kernels for 69%

profile of v3, /device:TPU:0, one launch (start us, length us, event | category | flops | bytes accessed | tf_op | source)
XLA Modules:
  0.0 211.5 jit_solution(10469965237269133695)
XLA Ops:
  6.5 3.1 %pad_maximum_fusion = bf16[16,128,512]{2,1,0:T(8,128)(2,1)} fusion(bf16[16,128,256]{2,1,0:T(8,128)(2,1)} %param.11, bf16[16,128,256]{2,1,0:T(8,128)(2,1)} %param.10), kind=kLoop, calls=%fused_computation | loop fusion | flops 4194304 | bytes 4194304 | tf_op jit(solution)/shard_map/concatenate | solution.py:330
  9.6 0.0 copy-start
  9.6 7.4 %all-to-all-start = ((bf16[16,128,512]{2,1,0:T(8,128)(2,1)}), bf16[16,128,512]{2,1,0:T(8,128)(2,1)S(1)}, u32[]{:S(2)}, u32[]{:S(2)}) async-start(bf16[16,128,512]{2,1,0:T(8,128)(2,1)} %pad_maximum_fusion), calls=%async_computation | async-start | bytes 4194304 | tf_op jit(solution)/shard_map/all_to_all | solution.py:331
  17.0 0.0 all-gather.2.cloned.1.call-start
  17.0 0.7 all-gather.2.cloned.1.call-update
  17.7 0.0 copy-done
  17.8 0.7 fusion.4
  18.4 2.6 %pad_add_fusion.node_ref = s32[3]{0:T(128)} fusion(s32[1]{0:T(128)} %bitcast.2, s32[1]{0:T(128)} %bitcast.1, s32[1]{0:T(128)} %bitcast), kind=kLoop, calls=%fused_computation.5 | loop fusion | flops 6 | bytes 24 | tf_op jit(solution)/shard_map/stack | solution.py:340
  21.0 38.0 %shard_map.82 = (f32[128,512]{1,0:T(8,128)}, f32[128,384]{1,0:T(8,128)}, f32[128,256]{1,0:T(8,128)}) custom-call(s32[2]{0:T(128)} %rank_ref.3, s32[2]{0:T(128)} %trunc_ref.3, s32[3]{0:T(128)} %pad_add_fusion.node_ref, bf16[2,1024,256]{2,1,0:T(8,128)(2,1)} %gen_ref.1, bf16[2,1024,256]{2,1,0:T(8,128)(2,1)} %upd_ref.1), custom_call_target="tpu_custom_call" | custom-call | flops 49999998976 | bytes 100000000 | tf_op jit(solution)/shard_map/pallas_call | solution.py:295
  58.9 17.6 %all-to-all-done = bf16[16,128,512]{2,1,0:T(8,128)(2,1)S(1)} async-done(((bf16[16,128,512]{2,1,0:T(8,128)(2,1)}), bf16[16,128,512]{2,1,0:T(8,128)(2,1)S(1)}, u32[]{:S(2)}, u32[]{:S(2)}) %all-to-all-start) | async-done | bytes 2097184 | tf_op jit(solution)/shard_map/all_to_all | solution.py:331
  76.5 0.2 copy.9
  76.7 1.5 fusion.3
  78.2 108.6 %shard_map.83 = f32[512,512]{1,0:T(8,128)} custom-call(s32[2]{0:T(128)} %rank_ref.3, s32[2]{0:T(128)} %trunc_ref.3, s32[3]{0:T(128)} %pad_add_fusion.node_ref, bf16[2,1024,256]{2,1,0:T(8,128)(2,1)} %get-tuple-element.12.gen_ref, bf16[2,1024,256]{2,1,0:T(8,128)(2,1)} %get-tuple-element.11.upd_ref, f32[128,512]{1,0:T(8,128)} %get-tuple-element.8.refs_0_, ...), custom_call_target="tpu_custom_call" | custom-call | flops 49999998976 | bytes 100000000 | tf_op jit(solution)/shard_map/pallas_call | solution.py:308
  186.8 0.1 collective-permute-start.1
  186.9 0.0 all-gather.2.cloned.1.call-done
  186.9 2.0 fusion
  189.0 1.7 collective-permute-start
  190.6 7.0 %collective-permute-done = f32[128,512]{1,0:T(8,128)S(1)} collective-permute-done((f32[128,512]{1,0:T(8,128)S(1)}, f32[128,512]{1,0:T(8,128)S(1)}, u32[]{:S(2)}, u32[]{:S(2)}) %collective-permute-start) | collective-permute-done | bytes 262176 | tf_op jit(solution)/shard_map/ppermute | solution.py:324
  197.7 0.0 collective-permute-done.1
  197.7 1.2 convolution_multiply_fusion
  198.9 1.7 collective-permute-start.2
  200.6 3.4 %collective-permute-done.2 = f32[64,512]{1,0:T(8,128)S(1)} collective-permute-done((f32[64,512]{1,0:T(8,128)S(1)}, f32[64,512]{1,0:T(8,128)S(1)}, u32[]{:S(2)}, u32[]{:S(2)}) %collective-permute-start.2) | collective-permute-done | bytes 131104 | tf_op jit(solution)/shard_map/ppermute | solution.py:324
  204.0 0.7 slice_select_fusion
  (1 shorter events, 0.0 us)
Async XLA Ops:
  9.6 8.2 %copy-start = (s32[4,14]{1,0:T(4,128)S(1)}, s32[4,14]{1,0:T(4,128)}, u32[]{:S(2)}) copy-start(s32[4,14]{1,0:T(4,128)} %param.14) | copy-start | bytes 676
  9.6 66.9 %all-to-all-start = ((bf16[16,128,512]{2,1,0:T(8,128)(2,1)}), bf16[16,128,512]{2,1,0:T(8,128)(2,1)S(1)}, u32[]{:S(2)}, u32[]{:S(2)}) async-start(bf16[16,128,512]{2,1,0:T(8,128)(2,1)} %pad_maximum_fusion), calls=%async_computation | async-start | bytes 4194304 | tf_op jit(solution)/shard_map/all_to_all | solution.py:331
  17.0 169.9 %all-gather.2.cloned.1.call-start = ((), (), s32[]{:S(2)}) async-start(), calls=%async_computation.1 | async-start | bytes 1179648 | tf_op jit(solution)/shard_map/all_gather | solution.py:334
  186.8 10.9 %collective-permute-start.1 = (f32[512,512]{1,0:T(8,128)}, f32[512,512]{1,0:T(8,128)S(1)}, u32[]{:S(2)}, u32[]{:S(2)}) collective-permute-start(f32[512,512]{1,0:T(8,128)} %shard_map.83), channel_id=1, source_target_pairs={{0,8},{8,0},{16,24},{24,16},{1,9},{9,1},{17,25},{25,17},{2,10},{10... | collective-permute-start | bytes 3145736 | tf_op jit(solution)/shard_map/ppermute | solution.py:324
  189.0 8.7 %collective-permute-start = (f32[128,512]{1,0:T(8,128)S(1)}, f32[128,512]{1,0:T(8,128)S(1)}, u32[]{:S(2)}, u32[]{:S(2)}) collective-permute-start(f32[128,512]{1,0:T(8,128)S(1)} %fusion), channel_id=1, source_target_pairs={{0,1},{1,0},{2,3},{3,2},{4,5},{5,4},{6,7},{7,6},{8,9},{9,8},{10,11... | collective-permute-start | bytes 786440 | tf_op jit(solution)/shard_map/ppermute | solution.py:324
  198.9 5.1 %collective-permute-start.2 = (f32[64,512]{1,0:T(8,128)S(1)}, f32[64,512]{1,0:T(8,128)S(1)}, u32[]{:S(2)}, u32[]{:S(2)}) collective-permute-start(f32[64,512]{1,0:T(8,128)S(1)} %slice.19), channel_id=1, source_target_pairs={{0,1},{1,0},{2,3},{3,2},{4,5},{5,4},{6,7},{7,6},{8,9},{9,8},{10,11... | collective-permute-start | bytes 393224 | tf_op jit(solution)/shard_map/ppermute | solution.py:324
Sparse Core Ops, SparseCore 0:
  19.9 58.9 all-gather.1
